TPU v7x, 32 devices: a whole 2x2x4 slice. The times are simulated.
32 devices in a mesh: row: 16 (over z, y, core), col: 2 (over x).
Axes of the slice: x: 2, y: 2, z: 4, core: 2. Of those that a mesh axis runs over, the one named last changes fastest.
Arguments:
- queries: bfloat16 [128, 64, 2240], P('row', 'col'), may hold values from -6 to 6
- keys: bfloat16 [128, 64, 2240], P('row', 'col'), may hold values from -120 to 120
- values: bfloat16 [128, 64, 2240], P('row', 'col'), may hold values from -10 to 10
- features: bfloat16 [128, 64, 11200], P('row', 'col'), may hold values from -6 to 6
- conv_weight: bfloat16 [3, 3, 11200], replicated, may hold values from -2 to 2
- conv_bias: bfloat16 [11200], replicated, may hold values from -3 to 3
Outputs:
- attended: bfloat16 [128, 64, 2240], P('row', 'col')
- gated: bfloat16 [128, 64, 5600], P('row', 'col')
All inputs are finite; a program needn't handle non-finite values.
Results may differ from a plain program's by a relative error of at most 0.001.
Values may be sent and summed in bfloat16 or wider, within the bound.
No kernel may reach another device: no remote copies, remote signals or barrier semaphores. Data moves between devices by JAX's collectives and lax.ppermute only.
A program may use at most 128 MiB of HBM per device.

v0:
```python
import jax
import jax.numpy as jnp
from jax import lax
from jax.sharding import PartitionSpec as P

HEADS = 70
HEAD_DIM = 32
HID = 5600


def padded_2(block, sides, width):
    for axis, dim in sides:
        count = lax.axis_size(axis)
        forward = [(i, i + 1) for i in range(count - 1)]
        backward = [(target, source) for source, target in forward]
        low = lax.ppermute(
            lax.slice_in_dim(block, block.shape[dim] - width, None, axis=dim), axis, forward
        )
        high = lax.ppermute(lax.slice_in_dim(block, 0, width, axis=dim), axis, backward)
        block = jnp.concatenate([low, block, high], axis=dim)
    return block


def on_device(queries, keys, values, features, conv_weight, conv_bias):
    tile_rows, tile_cols, channels = queries.shape
    key_heads = jnp.maximum(keys.reshape(-1, HEADS, HEAD_DIM), 0)
    value_heads = values.reshape(-1, HEADS, HEAD_DIM)
    local_state = jnp.einsum(
        "thj,thi->jhi", value_heads, key_heads, preferred_element_type=jnp.float32
    ).reshape(HEAD_DIM, channels)
    local_keys = jnp.sum(key_heads, axis=0, dtype=jnp.float32).reshape(1, channels)
    state_sum, key_sum = lax.psum((local_state, local_keys), ("row", "col"))
    kv_state = state_sum.reshape(HEAD_DIM, HEADS, HEAD_DIM)
    key_total = key_sum.reshape(HEADS, HEAD_DIM)
    query_heads = jnp.maximum(queries.reshape(-1, HEADS, HEAD_DIM), 0).astype(jnp.float32)
    numerator = jnp.einsum("thi,jhi->thj", query_heads, kv_state, precision=lax.Precision.HIGHEST)
    denominator = jnp.einsum("thi,hi->th", query_heads, key_total, precision=lax.Precision.HIGHEST)
    attended = (
        (numerator / (denominator[:, :, None] + 1e-15))
        .astype(jnp.bfloat16)
        .reshape(tile_rows, tile_cols, channels)
    )
    padded = padded_2(features, (("row", 0), ("col", 1)), 1)
    weight_float = conv_weight.astype(jnp.float32)
    conv_sum = conv_bias.astype(jnp.float32)
    for tap_row in range(3):
        for tap_col in range(3):
            window = padded[tap_row : tap_row + tile_rows, tap_col : tap_col + tile_cols]
            conv_sum = conv_sum + weight_float[tap_row, tap_col] * window.astype(jnp.float32)
    gated = (conv_sum[:, :, :HID] * jax.nn.silu(conv_sum[:, :, HID:])).astype(jnp.bfloat16)
    return (attended, gated)


def solution(mesh):
    return jax.shard_map(
        on_device,
        mesh=mesh,
        in_specs=(
            P("row", "col", None),
            P("row", "col", None),
            P("row", "col", None),
            P("row", "col", None),
            P(),
            P(),
        ),
        out_specs=(P("row", "col", None), P("row", "col", None)),
        check_vma=False,
    )
```

profile of v0, /device:TPU:0, one launch (start us, length us, event | category | flops | bytes accessed | tf_op | source)
XLA Modules:
  0.0 248.3 jit_solution(16774100580679525855)
XLA Ops:
  7.2 0.0 copy-start.6
  7.2 0.0 all-reduce.2.cloned.1.call-start
  7.2 2.4 fusion.13
  9.6 3.2 %collective-permute-start = (bf16[1,32,11200]{2,1,0:T(8,128)(2,1)S(1)}, bf16[1,32,11200]{2,1,0:T(8,128)(2,1)}, u32[]{:S(2)}, u32[]{:S(2)}) collective-permute-start(bf16[1,32,11200]{2,1,0:T(8,128)(2,1)S(1)} %get-tuple-element.14), channel_id=1, source_target_pairs={{0,2},{2,4},{4,6},{6,8},{8,10},{10,12},{12,14},{14,16},{16,18},{18... | collective-permute-start | bytes 2150408 | tf_op jit(solution)/shard_map/ppermute | solution.py:16
  12.8 1.3 collective-permute-start.1
  14.1 1.4 broadcast_maximum_fusion.1
  15.4 5.0 %reshape.43 = bf16[256,70,32]{2,1,0:T(8,128)(2,1)} reshape(bf16[8,32,2240]{2,1,0:T(8,128)(2,1)S(1)} %broadcast_maximum_fusion.1) | data formatting | bytes 2293760 | tf_op jit(solution)/shard_map/max | solution.py:26
  20.5 0.0 copy-done.6
  20.5 4.9 %reshape.44 = bf16[256,70,32]{2,1,0:T(8,128)(2,1)} reshape(bf16[8,32,2240]{2,1,0:T(8,128)(2,1)S(1)} %copy-done.6) | data formatting | bytes 2293760 | tf_op jit(solution)/shard_map/reshape | solution.py:27
  25.4 6.3 %fusion.5 = f32[32,70,32]{0,2,1:T(8,128)} fusion(bf16[256,70,32]{2,1,0:T(8,128)(2,1)} %reshape.44, bf16[256,70,32]{2,1,0:T(8,128)(2,1)} %reshape.43), kind=kOutput, calls=%fused_computation.13 | convolution fusion | flops 36700160 | bytes 2580480 | tf_op jit(solution)/shard_map/thj,thi->jhi/dot_general | solution.py:28
  31.7 0.0 all-reduce.2.cloned.1.call-update
  31.8 0.0 copy-done.7
  31.8 1.0 fusion.14
  32.7 0.0 copy-done.5
  32.7 0.1 broadcast_maximum_fusion
  32.8 0.0 copy-start.15
  32.8 8.3 %copy.31 = bf16[8,32,11200]{2,0,1:T(8,128)(2,1)} copy(bf16[8,32,11200]{2,1,0:T(8,128)(2,1)} %param.9) | data formatting | bytes 11468800 | tf_op args[3]
  41.1 0.0 copy-done.15
  41.1 0.0 copy-start.2
  41.1 4.9 %reshape.45 = bf16[256,70,32]{2,1,0:T(8,128)(2,1)} reshape(bf16[8,32,2240]{2,1,0:T(8,128)(2,1)S(1)} %broadcast_maximum_fusion) | data formatting | bytes 2293760 | tf_op jit(solution)/shard_map/max | solution.py:35
  46.1 6.1 %copy.45 = bf16[256,70,32]{0,2,1:T(8,128)(2,1)S(1)} copy(bf16[256,70,32]{2,1,0:T(8,128)(2,1)} %reshape.45) | data formatting | bytes 2293760 | tf_op jit(solution)/shard_map/max | solution.py:35
  52.2 0.3 convert_reduce_fusion
  52.4 0.1 reshape.37
  52.5 43.5 %psum.15 = f32[70,32]{1,0:T(8,128)S(1)} all-reduce(f32[70,32]{1,0:T(8,128)S(1)} %reshape.37), channel_id=1, replica_groups=mesh['row'=16,'col'=2] {'row','col'}, use_global_device_ids=true, to_apply=%region_2.0 | all-reduce | flops 2240 | bytes 17920 | tf_op jit(solution)/shard_map/psum | solution.py:32
  96.0 0.6 fusion.11
  96.6 0.6 fusion.10
  97.3 0.0 collective-permute-done
  97.3 2.2 copy.30
  99.5 0.0 copy-start.4
  99.5 0.0 copy-start.14
  99.5 0.0 collective-permute-done.1
  99.5 2.3 copy.32
  101.8 0.0 copy-start
  101.9 1.1 copy-done
  102.9 2.1 pad_maximum_fusion.5
  105.0 4.9 %collective-permute-start.2 = (bf16[10,1,11200]{2,0,1:T(8,128)(2,1)}, bf16[10,1,11200]{2,0,1:T(8,128)(2,1)}, u32[]{:S(2)}, u32[]{:S(2)}) collective-permute-start(bf16[10,1,11200]{2,0,1:T(8,128)(2,1)} %get-tuple-element.12), channel_id=1, source_target_pairs={{0,1},{2,3},{4,5},{6,7},{8,9},{10,11},{12,13},{14,15},{16,17},{18,... | collective-permute-start | bytes 672008 | tf_op jit(solution)/shard_map/ppermute | solution.py:16
  109.9 1.3 collective-permute-start.3
  111.2 55.4 %all-reduce.2.cloned.1.call-done = f32[32,70,32]{0,2,1:T(8,128)} async-done(((f32[32,70,32]{0,2,1:T(8,128)}), f32[32,70,32]{0,2,1:T(8,128)}) %all-reduce.2.cloned.1.call-update) | async-done | bytes 286736 | tf_op jit(solution)/shard_map/psum | solution.py:32
  166.6 0.0 copy-done.4
  166.6 3.4 %fusion.4 = bf16[256,70,32]{0,2,1:T(8,128)(2,1)} fusion(f32[32,70,32]{0,2,1:T(8,128)} %all-reduce.2.cloned.1.call-done, bf16[256,70,32]{0,2,1:T(8,128)(2,1)S(1)} %copy-done.4, f32[256,70]{0,1:T(8,128)S(1)} %copy-done.14), kind=kOutput, calls=%fused_computation.12 | convolution fusion | flops 221347840 | bytes 2652160 | tf_op jit(solution)/shard_map/thi,jhi->thj/dot_general | solution.py:36
  170.0 6.0 %reshape.38 = bf16[8,32,2240]{1,0,2:T(8,128)(2,1)} reshape(bf16[256,70,32]{0,2,1:T(8,128)(2,1)} %fusion.4) | data formatting | bytes 2293760 | tf_op jit(solution)/shard_map/reshape | solution.py:41
  176.1 6.3 %copy.38 = bf16[8,32,2240]{2,1,0:T(8,128)(2,1)} copy(bf16[8,32,2240]{1,0,2:T(8,128)(2,1)} %reshape.38) | data formatting | bytes 2293760
  182.4 0.0 collective-permute-done.2
  182.4 0.0 collective-permute-done.3
  182.5 22.1 %maximum_maximum_fusion = (bf16[10,33,11200]{2,0,1:T(8,128)(2,1)}, bf16[10,33,11200]{2,0,1:T(8,128)(2,1)}) fusion(bf16[1,32,11200]{2,0,1:T(2,128)(2,1)} %copy-done, bf16[8,32,11200]{2,0,1:T(8,128)(2,1)} %copy.31, bf16[1,32,11200]{2,0,1:T(2,128)(2,1)S(1)} %copy.30, bf16[10,1,11200]{2,0,1:T(8,128)(2,1)} %collective-permute-done.2, ...), kind=kLoop, calls=%fused_computation | loop fusion | flops 59136000 | bytes 22400000 | tf_op jit(solution)/shard_map/concatenate | solution.py:20
  204.7 29.1 %multiply_add_fusion = f32[8,32,11200]{2,0,1:T(8,128)} fusion(bf16[8,32,11200]{2,0,1:T(8,128)(2,1)S(1)} %bitcast.28, bf16[10,33,11200]{2,0,1:T(8,128)(2,1)} %get-tuple-element.11, bf16[1,32,11200]{2,0,1:T(2,128)(2,1)S(1)} %copy-done.1, bf16[10,33,11200]{2,0,1:T(8,128)(2,1)} %get-tuple-element.10, bf16[1,32,11200]{2,0,1:T(2,128)(2,1)S(1)} %copy.30, ...), kind=kLoop, calls=%fused_computation.2 | loop fusion | flops 94617600 | bytes 53491200 | tf_op jit(solution)/shard_map/add | solution.py:49
  233.8 5.2 %fusion = bf16[8,32,5600]{2,0,1:T(8,128)(2,1)S(1)} fusion(f32[8,32,11200]{2,0,1:T(8,128)} %multiply_add_fusion), kind=kLoop, calls=%fused_computation.4 | loop fusion | flops 8601600 | bytes 14336000 | tf_op jit(solution)/shard_map/convert_element_type | solution.py:50
  239.1 2.4 copy.39
  (26 shorter events, 0.1 us)
Async XLA Ops:
  7.2 13.3 %copy-start.6 = (bf16[8,32,2240]{2,1,0:T(8,128)(2,1)S(1)}, bf16[8,32,2240]{2,1,0:T(8,128)(2,1)}, u32[]{:S(2)}) copy-start(bf16[8,32,2240]{2,1,0:T(8,128)(2,1)} %param.8) | copy-start | bytes 3440644
  7.2 159.4 %all-reduce.2.cloned.1.call-start = ((), (), s32[]{:S(2)}) async-start(), calls=%async_computation | async-start | bytes 2293760 | tf_op jit(solution)/shard_map/psum | solution.py:32
  9.6 87.7 %collective-permute-start = (bf16[1,32,11200]{2,1,0:T(8,128)(2,1)S(1)}, bf16[1,32,11200]{2,1,0:T(8,128)(2,1)}, u32[]{:S(2)}, u32[]{:S(2)}) collective-permute-start(bf16[1,32,11200]{2,1,0:T(8,128)(2,1)S(1)} %get-tuple-element.14), channel_id=1, source_target_pairs={{0,2},{2,4},{4,6},{6,8},{8,10},{10,12},{12,14},{14,16},{16,18},{18... | collective-permute-start | bytes 2150408 | tf_op jit(solution)/shard_map/ppermute | solution.py:16
  12.8 86.7 %collective-permute-start.1 = (bf16[1,32,11200]{2,1,0:T(8,128)(2,1)}, bf16[1,32,11200]{2,1,0:T(8,128)(2,1)}, u32[]{:S(2)}, u32[]{:S(2)}) collective-permute-start(bf16[1,32,11200]{2,1,0:T(8,128)(2,1)} %get-tuple-element.15), channel_id=1, source_target_pairs={{2,0},{4,2},{6,4},{8,6},{10,8},{12,10},{14,12},{16,14},{18,16},{20... | collective-permute-start | bytes 2150408 | tf_op jit(solution)/shard_map/ppermute | solution.py:19
  25.4 6.4 %copy-start.7 = (bf16[3,3,11200]{2,1,0:T(4,128)(2,1)S(1)}, bf16[3,3,11200]{2,1,0:T(4,128)(2,1)}, u32[]{:S(2)}) copy-start(bf16[3,3,11200]{2,1,0:T(4,128)(2,1)} %param.10) | copy-start | bytes 604804
  25.4 7.3 %copy-start.5 = (bf16[8,32,2240]{2,1,0:T(8,128)(2,1)S(1)}, bf16[8,32,2240]{2,1,0:T(8,128)(2,1)}, u32[]{:S(2)}) copy-start(bf16[8,32,2240]{2,1,0:T(8,128)(2,1)} %param.6) | copy-start | bytes 3440644
  32.8 8.3 %copy-start.15 = (bf16[11200]{0:T(1024)(128)(2,1)S(1)}, bf16[11200]{0:T(1024)(128)(2,1)}, u32[]{:S(2)}) copy-start(bf16[11200]{0:T(1024)(128)(2,1)} %param.11) | copy-start | bytes 67204
  41.1 11.0 %copy-start.2 = (bf16[8,32,2240]{2,1,0:T(8,128)(2,1)S(1)}, bf16[8,32,2240]{2,1,0:T(8,128)(2,1)}, u32[]{:S(2)}) copy-start(bf16[8,32,2240]{2,1,0:T(8,128)(2,1)} %param.7) | copy-start | bytes 3440644
  52.2 45.1 %copy-start.3 = (bf16[256,70,32]{0,2,1:T(8,128)(2,1)}, bf16[256,70,32]{0,2,1:T(8,128)(2,1)S(1)}, u32[]{:S(2)}) copy-start(bf16[256,70,32]{0,2,1:T(8,128)(2,1)S(1)} %copy.45) | copy-start | bytes 3440644
  99.5 67.1 %copy-start.4 = (bf16[256,70,32]{0,2,1:T(8,128)(2,1)S(1)}, bf16[256,70,32]{0,2,1:T(8,128)(2,1)}, u32[]{:S(2)}) copy-start(bf16[256,70,32]{0,2,1:T(8,128)(2,1)} %copy-done.3) | copy-start | bytes 3440644
  99.5 67.1 %copy-start.14 = (f32[256,70]{0,1:T(8,128)S(1)}, f32[256,70]{0,1:T(8,128)}, u32[]{:S(2)}) copy-start(f32[256,70]{0,1:T(8,128)} %fusion.10) | copy-start | bytes 215044
  101.8 1.1 copy-start
  105.0 77.4 %collective-permute-start.2 = (bf16[10,1,11200]{2,0,1:T(8,128)(2,1)}, bf16[10,1,11200]{2,0,1:T(8,128)(2,1)}, u32[]{:S(2)}, u32[]{:S(2)}) collective-permute-start(bf16[10,1,11200]{2,0,1:T(8,128)(2,1)} %get-tuple-element.12), channel_id=1, source_target_pairs={{0,1},{2,3},{4,5},{6,7},{8,9},{10,11},{12,13},{14,15},{16,17},{18,... | collective-permute-start | bytes 672008 | tf_op jit(solution)/shard_map/ppermute | solution.py:16
  109.9 72.5 %collective-permute-start.3 = (bf16[10,1,11200]{2,0,1:T(8,128)(2,1)S(1)}, bf16[10,1,11200]{2,0,1:T(8,128)(2,1)}, u32[]{:S(2)}, u32[]{:S(2)}) collective-permute-start(bf16[10,1,11200]{2,0,1:T(8,128)(2,1)S(1)} %get-tuple-element.13), channel_id=1, source_target_pairs={{1,0},{3,2},{5,4},{7,6},{9,8},{11,10},{13,12},{15,14},{17,16},{19,... | collective-permute-start | bytes 672008 | tf_op jit(solution)/shard_map/ppermute | solution.py:19
  176.0 28.5 %slice-start = ((s8[5767168]{0:T(1024)(128)(4,1)}), s8[1572864]{0:T(1024)(128)(4,1)S(1)}, s32[]{:S(2)}) async-start(s8[5767168]{0:T(1024)(128)(4,1)} %bitcast.27), calls=%async_computation.1 | async-start | bytes 3145728
  182.4 22.2 %slice-start.1 = ((s8[5767168]{0:T(1024)(128)(4,1)}), s8[4194304]{0:T(1024)(128)(4,1)S(1)}, s32[]{:S(2)}) async-start(s8[5767168]{0:T(1024)(128)(4,1)} %bitcast.27), calls=%async_computation.2 | async-start | bytes 8388608
  182.4 22.2 %copy-start.1 = (bf16[1,32,11200]{2,0,1:T(2,128)(2,1)S(1)}, bf16[1,32,11200]{2,0,1:T(2,128)(2,1)}, u32[]{:S(2)}) copy-start(bf16[1,32,11200]{2,0,1:T(2,128)(2,1)} %copy-done) | copy-start | bytes 2150404
  182.4 22.2 %copy-start.8 = (f32[1,1,11200]{2,1,0:T(1,128)S(1)}, f32[1,1,11200]{2,1,0:T(1,128)}, u32[]{:S(2)}) copy-start(f32[1,1,11200]{2,1,0:T(1,128)} %get-tuple-element.19) | copy-start | bytes 134404
  182.4 22.2 %copy-start.9 = (f32[1,1,11200]{2,1,0:T(1,128)S(1)}, f32[1,1,11200]{2,1,0:T(1,128)}, u32[]{:S(2)}) copy-start(f32[1,1,11200]{2,1,0:T(1,128)} %get-tuple-element.20) | copy-start | bytes 134404
  182.4 22.2 %copy-start.10 = (f32[1,1,11200]{2,1,0:T(1,128)S(1)}, f32[1,1,11200]{2,1,0:T(1,128)}, u32[]{:S(2)}) copy-start(f32[1,1,11200]{2,1,0:T(1,128)} %get-tuple-element.21) | copy-start | bytes 134404
  182.4 22.2 %copy-start.11 = (f32[1,1,11200]{2,1,0:T(1,128)S(1)}, f32[1,1,11200]{2,1,0:T(1,128)}, u32[]{:S(2)}) copy-start(f32[1,1,11200]{2,1,0:T(1,128)} %get-tuple-element.22) | copy-start | bytes 134404
  182.4 22.2 %copy-start.12 = (f32[1,1,11200]{2,1,0:T(1,128)S(1)}, f32[1,1,11200]{2,1,0:T(1,128)}, u32[]{:S(2)}) copy-start(f32[1,1,11200]{2,1,0:T(1,128)} %get-tuple-element.23) | copy-start | bytes 134404
  182.4 22.2 %copy-start.13 = (f32[1,1,11200]{2,1,0:T(1,128)S(1)}, f32[1,1,11200]{2,1,0:T(1,128)}, u32[]{:S(2)}) copy-start(f32[1,1,11200]{2,1,0:T(1,128)} %get-tuple-element.24) | copy-start | bytes 134404
Sparse Core Ops, SparseCore 0:
  31.9 134.6 all-reduce.1
where the time goes:
time: 249 us; the launch traced here: 248 us
  other arithmetic  60.9 us (24%)
  waiting for transfers between devices  55.4 us (22%)
  local copies, waits for them, and re-layouts  53.1 us (21%)
  blocking collectives  43.5 us (17%)
  between operations  14.3 us (6%)
  starting transfers between devices  10.7 us (4%)
  matrix products  10.4 us (4%)
    psum x1, waiting for transfers between devices, on_device(): state_sum, key_sum = lax.psum((local_state, local_keys), ('row', 'col'))  55.4 us
    psum x1, blocking collectives, on_device(): state_sum, key_sum = lax.psum((local_state, local_keys), ('row', 'col'))  43.5 us
    add x1, other arithmetic, on_device(): conv_sum + weight_float[tap_row, tap_col] * window.astype(jnp.float32)  29.1 us
    concatenate x1, other arithmetic, padded_2(): block = jnp.concatenate([low, block, high], axis=dim)  22.1 us
    unnamed x39, local copies, waits for them, and re-layouts  18.2 us
    max x2, local copies, waits for them, and re-layouts, on_device(): jnp.maximum(queries.reshape(-1, HEADS, HEAD_DIM), 0).astype(jnp.float32)  11 us
    ppermute x2, starting transfers between devices, padded_2(): lax.ppermute(lax.slice_in_dim(block, block.shape[dim] - width, None, axis...  8.08 us
    dot_general x1, matrix products, on_device(): jnp.einsum('thj,thi->jhi', value_heads, key_heads, preferred_element_type...  6.32 us
  transfers between devices with their start and end apart: 5, of which 1 were waited for; matrix products, arithmetic and copies ran while one was open for 25% of the time, Pallas kernels for 0%

commit v1 on v0

v1 whole, which is shorter than its diff:
```python
import functools
import jax
import jax.numpy as jnp
from jax import lax
from jax.experimental import pallas as pl
from jax.experimental.pallas import tpu as pltpu
from jax.sharding import PartitionSpec as P

HEAD_DIM = 32
LANES = 128
WIDE = 768
PAIR = 256
SUBLANES = 16
SMALL = pl.CostEstimate(flops=1024, bytes_accessed=1024, transcendentals=0)


def halves(channels):
    tiles = pl.cdiv(channels, LANES)
    per = pl.cdiv(tiles, 2)
    return tiles, per, pl.cdiv(per * (HEAD_DIM + 1), 8) * 8


def same_head(size):
    row_head = lax.broadcasted_iota(jnp.int32, (size, size), 0) // HEAD_DIM
    col_head = lax.broadcasted_iota(jnp.int32, (size, size), 1) // HEAD_DIM
    return row_head == col_head


def state_kernel(channels, place, k_ref, v_ref, features, mine, other, far, *refs):
    edge, *refs = refs if len(refs) == 5 else (None, *refs)
    packed, row, *refs = refs
    beside, sem = refs if len(refs) == 2 else (None, *refs)
    tiles, per, rows = halves(channels)
    step = pl.program_id(0)
    core = place[0]
    tokens = k_ref.shape[0] * k_ref.shape[1]
    tile_rows, tile_cols, width = features.shape
    copies = [pltpu.make_async_copy(features.at[(tile_rows - 1) * core], row, sem.at[0])]
    store = pltpu.make_async_copy(row, far.at[0], sem.at[1])
    if edge is not None:
        start = pl.multiple_of((tile_cols - SUBLANES) * (1 - place[1]), SUBLANES)
        copies.append(
            pltpu.make_async_copy(features.at[:, pl.ds(start, SUBLANES)], beside, sem.at[2])
        )

    @pl.when(step == 0)
    def _():
        for copy in copies:
            copy.start()
        packed[...] = jnp.zeros_like(packed)

    mask = same_head(PAIR)
    ones = jnp.ones((8, tokens), jnp.bfloat16)
    for part in range(WIDE // PAIR):
        at = slice(part * PAIR, (part + 1) * PAIR)
        keys = jnp.maximum(k_ref[:, :, at].reshape(tokens, PAIR), 0)
        values = v_ref[:, :, at].reshape(tokens, PAIR)
        product = lax.dot_general(
            values, keys, (((0,), (0,)), ((), ())), preferred_element_type=jnp.float32
        )
        product = jnp.where(mask, product, 0.0)
        state = product[:HEAD_DIM]
        for head in range(1, PAIR // HEAD_DIM):
            state = state + product[head * HEAD_DIM : (head + 1) * HEAD_DIM]
        total = jnp.dot(ones, keys, preferred_element_type=jnp.float32)
        for side in range(PAIR // LANES):
            tile = (step * (WIDE // PAIR) + part) * (PAIR // LANES) + side
            lanes = slice(side * LANES, (side + 1) * LANES)

            @pl.when(tile < tiles)
            def _():
                half, spot = tile // per, tile % per
                begin = pl.multiple_of(spot * HEAD_DIM, HEAD_DIM)
                packed[half, pl.ds(begin, HEAD_DIM), :] = state[:, lanes]
                packed[half, pl.ds(per * HEAD_DIM + spot, 1), :] = total[:1, lanes]

    @pl.when(step == pl.num_programs(0) - 1)
    def _():
        mine[...] = packed[core]
        other[...] = packed[1 - core]

        store.wait()

    @pl.when(step == 1)
    def _():
        copies[0].wait()
        store.start()

    if edge is not None:

        @pl.when(step == 1)
        def _():
            copies[1].wait()

            @pl.when(place[1] == 0)
            def _():
                edge[...] = beside[:, SUBLANES - 1, :]

            @pl.when(place[1] != 0)
            def _():
                edge[...] = beside[:, 0, :]


def local_state(place, keys, values, features, with_edge):
    tile_rows, tile_cols, channels = keys.shape
    width = features.shape[2]
    rows = halves(channels)[2]
    block = pl.BlockSpec((tile_rows, tile_cols, WIDE), lambda i, c: (0, 0, i))
    shapes = [jax.ShapeDtypeStruct((rows, LANES), jnp.float32)] * 2
    scratch = [pltpu.VMEM((2, rows, LANES), jnp.float32)]
    shapes.append(pltpu.HBM((1, tile_cols, width), features.dtype))
    scratch.append(pltpu.VMEM((tile_cols, width), features.dtype))
    if with_edge:
        shapes.append(jax.ShapeDtypeStruct((tile_rows, width), features.dtype))
        scratch.append(pltpu.VMEM((tile_rows, SUBLANES, width), features.dtype))
    return pl.pallas_call(
        functools.partial(state_kernel, channels),
        out_shape=shapes,
        grid_spec=pltpu.PrefetchScalarGridSpec(
            num_scalar_prefetch=1,
            grid=(pl.cdiv(channels, WIDE),),
            in_specs=[block, block, pl.BlockSpec(memory_space=pl.ANY)],
            out_specs=[
                pl.BlockSpec(memory_space=pl.ANY if len(x.shape) == 3 else pltpu.VMEM) for x in shapes
            ],
            scratch_shapes=scratch + [pltpu.SemaphoreType.DMA((3,))],
        ),
        compiler_params=pltpu.CompilerParams(vmem_limit_bytes=8 << 20),
        cost_estimate=pl.CostEstimate(flops=1 << 29, bytes_accessed=64 << 20, transcendentals=0),
        name="local_state",
    )(place, *(pltpu.with_memory_space_constraint(x, pltpu.HBM) for x in (keys, values, features)))


def in_two(x):
    high = x.astype(jnp.bfloat16)
    return high, (x - high.astype(jnp.float32)).astype(jnp.bfloat16)


def attend_kernel(channels, place, q_ref, mine, other, ends, _, out, gated, packed, sem):
    tiles, per, rows = halves(channels)
    step = pl.program_id(0)
    core = place[0]
    tile_rows, tile_cols, _ = q_ref.shape
    tokens = tile_rows * tile_cols
    copies = [
        pltpu.make_async_copy(ends.at[k], gated.at[(tile_rows - 1) * low], sem.at[k])
        for k, low in enumerate((1 - core, core))
    ]

    @pl.when(step == 0)
    def _():
        for copy in copies:
            copy.start()
        packed[core] = mine[...]
        packed[1 - core] = other[...]

    mask = same_head(PAIR)
    lane = lax.broadcasted_iota(jnp.int32, (tokens, PAIR), 1)
    zero = jnp.zeros((), jnp.bfloat16)

    def weighted(queries, matrices):
        total = None
        for matrix in matrices:
            matrix = jnp.where(mask, matrix, zero)
            term = lax.dot_general(
                queries, matrix, (((1,), (1,)), ((), ())), preferred_element_type=jnp.float32
            )
            total = term if total is None else total + term
        return total

    for part in range(WIDE // PAIR):
        pair = step * (WIDE // PAIR) + part
        at = slice(part * PAIR, (part + 1) * PAIR)
        queries = jnp.maximum(q_ref[:, :, at].reshape(tokens, PAIR), 0)
        queries = jnp.where(lane < channels - pair * PAIR, queries, zero)
        states, totals = [], []
        for side in range(PAIR // LANES):
            tile = jnp.minimum(pair * (PAIR // LANES) + side, tiles - 1)
            half, place = tile // per, tile % per
            start = pl.multiple_of(place * HEAD_DIM, HEAD_DIM)
            states.append(packed[half, pl.ds(start, HEAD_DIM), :])
            totals.append(packed[half, pl.ds(per * HEAD_DIM + place, 1), :])
        state, total = jnp.concatenate(states, 1), jnp.concatenate(totals, 1)
        numerator = weighted(
            queries, [jnp.concatenate([x] * (PAIR // HEAD_DIM), 0) for x in in_two(state)]
        )
        denominator = weighted(queries, [jnp.broadcast_to(x, (PAIR, PAIR)) for x in in_two(total)])
        result = (numerator / (denominator + 1e-15)).astype(jnp.bfloat16)
        out[:, :, at] = result.reshape(tile_rows, tile_cols, PAIR)

    @pl.when(step == pl.num_programs(0) - 1)
    def _():
        for copy in copies:
            copy.wait()


def attend(place, queries, mine, other, ends, gated):
    tile_rows, tile_cols, channels = queries.shape
    rows = halves(channels)[2]
    block = pl.BlockSpec((tile_rows, tile_cols, WIDE), lambda i, c: (0, 0, i))
    half = pl.BlockSpec((rows, LANES), lambda i, c: (0, 0))
    anywhere = pl.BlockSpec(memory_space=pl.ANY)
    return pl.pallas_call(
        functools.partial(attend_kernel, channels),
        out_shape=[
            jax.ShapeDtypeStruct(x.shape, jnp.bfloat16) for x in (queries, gated)
        ],
        grid_spec=pltpu.PrefetchScalarGridSpec(
            num_scalar_prefetch=1,
            grid=(pl.cdiv(channels, WIDE),),
            in_specs=[block, half, half, pl.BlockSpec(memory_space=pltpu.VMEM), anywhere],
            out_specs=[block, anywhere],
            scratch_shapes=[
                pltpu.VMEM((2, rows, LANES), jnp.float32),
                pltpu.SemaphoreType.DMA((2,)),
            ],
        ),
        input_output_aliases={5: 1},
        compiler_params=pltpu.CompilerParams(vmem_limit_bytes=8 << 20),
        cost_estimate=SMALL,
        name="attend",
    )(place, queries, mine, other, ends, gated)


def widened(x):
    channel = lax.broadcasted_iota(jnp.int32, (1, x.shape[1]), 1)
    return x.astype(jnp.float32) * jnp.where(channel < x.shape[1] // 2, 1.0, 0.5)


def conv_kernel(targets, firsts, unroll, *refs):
    where, features, beside, *refs = refs
    if not targets:
        near, far, near_corner, far_corner, *refs = refs
        parts, refs = refs[: len(firsts)], refs[len(firsts) :]
        *refs, sem = refs
    weight, bias, out, *refs = refs
    copies = []
    if not targets:
        gated, *refs = refs
        for k, (start, part) in enumerate(zip(firsts, parts)):
            place = gated.at[pl.ds(start, part.shape[0])]
            copies.append(pltpu.make_async_copy(part, place, sem.at[k]))
            copies[-1].start()
    weights, biases, margins, sums, carry = refs
    tile_rows, tile_cols, channels = features.shape
    hidden = channels // 2
    tiles = pl.cdiv(hidden, LANES)
    first_gate = hidden // LANES
    shift = LANES - hidden % LANES
    count = len(targets) or 2
    last = tile_rows - 1
    core = where[0]
    if targets:
        first = targets[0] - 1
        sources = [(features, first + k) for k in range(count + 2)]
        triples = [(k, k + 1, k + 2) for k in range(count)]
        orders = [[0, 1, 2]] * count
    else:
        sources = [
            (near, 0), (features, (1 - core) * last), (features, 1 + (1 - core) * (last - 2)),
            (far, 0), (features, core * last), (features, 1 + core * (last - 2)),
        ]
        triples = [(0, 1, 2), (3, 4, 5)]
        orders = [[2 * (1 - core), 1, 2 * core], [2 * core, 1, 2 * (1 - core)]]

    for tap in range(3):
        weights[tap, :, :channels] = widened(weight[tap])
    biases[:, :channels] = widened(bias[...])
    for side in range(2):
        place = side * (beside.shape[0] - 1)
        keep = where[1 + side].astype(jnp.float32)
        edge = beside[place].astype(jnp.float32) * keep
        column = slice(2 * side, 2 * side + 1)
        if targets:
            rows = [edge[first + tap : first + tap + count] for tap in range(3)]
            margins[side, :, :channels] = sum(
                rows[tap] * weights[tap, column, :channels] for tap in range(3)
            )
            continue
        top = edge[:1], edge[1:2]
        bottom = edge[last:], edge[last - 1 : last]
        for target, corner in enumerate((near_corner, far_corner)):
            below = core == (1 if target else 0)
            rows = [corner[place : place + 1].astype(jnp.float32) * keep]
            rows += [jnp.where(below, low, high) for low, high in zip(bottom, top)]
            margins[side, target : target + 1, :channels] = sum(
                row * weights[tap, column, :channels] for row, tap in zip(rows, orders[target])
            )

    def span(tile):
        if isinstance(tile, int):
            return slice(tile * LANES, (tile + 1) * LANES)
        return pl.ds(pl.multiple_of(tile * LANES, LANES), LANES)

    def read(source, row, tile):
        if not isinstance(tile, int) or (tile + 1) * LANES <= channels:
            return source[row, :, span(tile)].astype(jnp.float32)
        part = source[row, :, tile * LANES :].astype(jnp.float32)
        fill = jnp.zeros((tile_cols, LANES - part.shape[1]), jnp.float32)
        return jnp.concatenate([part, fill], 1)

    def add_up(tile, buffer):
        at = span(tile)
        tokens = [read(source, row, tile) for source, row in sources]
        factors = [
            [[weights[tap, col : col + 1, at] for col in range(3)] for tap in order]
            for order in (orders[:1] if targets else orders)
        ]
        for target, triple in enumerate(triples):
            factor = factors[0 if targets else target]
            for col in (0, 2, 1):
                total = sum(factor[k][col] * tokens[triple[k]] for k in range(3))
                if col == 1:
                    total = total + biases[:, at]
                sums[buffer, target, col, 8 : 8 + tile_cols, :] = total
            sums[buffer, target, 0, 7:8, :] = margins[0, target : target + 1, at]
            sums[buffer, target, 2, 8 + tile_cols : 9 + tile_cols, :] = margins[1, target : target + 1, at]

    def collect(buffer, target):
        return (
            sums[buffer, target, 1, 8 : 8 + tile_cols, :]
            + sums[buffer, target, 0, 7 : 7 + tile_cols, :]
            + sums[buffer, target, 2, 9 : 9 + tile_cols, :]
        )

    def gate(buffer, target):
        x = collect(buffer, target)
        return pltpu.roll(x + x * jnp.tanh(x), shift, 1)

    lane = lax.broadcasted_iota(jnp.int32, (tile_cols, LANES), 1)

    def add_both(tile, step):
        add_up(tile + first_gate + 1, 2 * step)
        add_up(tile, 2 * step + 1)

    def finish(tile, step, before):
        at = span(tile)
        result = []
        for target in range(count):
            after = gate(2 * step, target)
            factor = jnp.where(lane < shift, before[target], after)
            product = (collect(2 * step + 1, target) * factor).astype(jnp.bfloat16)
            if isinstance(tile, int):
                size = min(hidden - tile * LANES, LANES)
                out[target, :, tile * LANES : tile * LANES + size] = product[:, :size]
            else:
                out[target, :, at] = product
            result.append(after)
        return result

    add_up(first_gate, 0)
    for target in range(count):
        carry[target] = gate(0, target)
    add_both(0, 0)

    full = tiles // unroll - 1

    @pl.loop(0, full)
    def _(i):
        before = [carry[target] for target in range(count)]
        for step in range(unroll):
            tile = i * unroll + step
            add_both(tile + 1, (step + 1) % unroll)
            before = finish(tile, step, before)
        for target in range(count):
            carry[target] = before[target]

    before = [carry[target] for target in range(count)]
    for tile in range(full * unroll, tiles):
        if tile + 1 < tiles:
            add_both(tile + 1, (tile + 1) % unroll)
        before = finish(tile, tile % unroll, before)

    for copy in copies:
        copy.wait()


def conv(targets, where, features, beside, halos, parts, firsts, weight, bias):
    tile_rows, tile_cols, channels = features.shape
    hidden = channels // 2
    count = len(targets) or 2
    unroll = 2 if targets else 4
    padded = pl.cdiv(channels, LANES) * LANES
    whole = pl.BlockSpec(memory_space=pltpu.VMEM)
    operands = [features, beside, *halos, *parts, weight, bias]
    shapes = [jax.ShapeDtypeStruct((count, tile_cols, hidden), jnp.bfloat16)]
    specs = [whole]
    scratch = [
        pltpu.VMEM((3, 3, padded), jnp.float32),
        pltpu.VMEM((1, padded), jnp.float32),
        pltpu.VMEM((2, count, padded), jnp.float32),
        pltpu.VMEM((2 * unroll, count, 3, tile_cols + 16, LANES), jnp.float32),
        pltpu.VMEM((count, tile_cols, LANES), jnp.float32),
    ]
    if not targets:
        shapes.append(jax.ShapeDtypeStruct((tile_rows, tile_cols, hidden), jnp.bfloat16))
        specs.append(pl.BlockSpec(memory_space=pl.ANY))
        scratch.append(pltpu.SemaphoreType.DMA((len(parts),)))
    return pl.pallas_call(
        functools.partial(conv_kernel, targets, firsts, unroll),
        out_shape=shapes,
        in_specs=[pl.BlockSpec(memory_space=pltpu.SMEM)] + [whole] * len(operands),
        out_specs=specs,
        scratch_shapes=scratch,
        compiler_params=pltpu.CompilerParams(vmem_limit_bytes=8 << 20),
        cost_estimate=SMALL,
        name="conv_rows" if targets else "conv_ends",
    )(where, *operands)


def near_kernel(place, features, near, sem):
    row = (features.shape[0] - 1) * (1 - place[0])
    copy = pltpu.make_async_copy(features.at[pl.ds(row, 1)], near, sem)
    copy.start()
    copy.wait()


def near_row(place, features):
    return pl.pallas_call(
        near_kernel,
        out_shape=pltpu.HBM((1, *features.shape[1:]), features.dtype),
        in_specs=[pl.BlockSpec(memory_space=pltpu.SMEM), pl.BlockSpec(memory_space=pltpu.VMEM)],
        out_specs=pl.BlockSpec(memory_space=pl.ANY),
        scratch_shapes=[pltpu.SemaphoreType.DMA],
        compiler_params=pltpu.CompilerParams(vmem_limit_bytes=8 << 20),
        cost_estimate=SMALL,
        name="near_row",
    )(place, features)


def swap(axis, bit):
    return [(i, i ^ bit) for i in range(lax.axis_size(axis))]


def together(*values):
    return lax.optimization_barrier(values)


def on_device(queries, keys, values, features, conv_weight, conv_bias):
    tile_rows, tile_cols, channels = features.shape
    rows, cols = lax.axis_size("row"), lax.axis_size("col")
    row, col = lax.axis_index("row"), lax.axis_index("col")
    core = (row % 2).astype(jnp.int32)
    place = jnp.stack([core, col]).astype(jnp.int32)
    where = jnp.stack([core, col > 0, col < cols - 1]).astype(jnp.int32)
    bias = conv_bias.reshape(1, -1)
    next_chip = [(i, i + 1) for i in range(1, rows - 1, 2)]
    next_chip += [(i + 1, i) for i, _ in next_chip]

    mine, other, far, *edges = local_state(place, keys, values, features, cols == 2)
    total = mine + lax.ppermute(other, "row", swap("row", 1))
    if cols == 2:
        beside = lax.ppermute(edges[0], "col", swap("col", 1))[None]
    else:
        right = [(i, i + 1) for i in range(cols - 1)]
        left = [(i + 1, i) for i in range(cols - 1)]
        beside = jnp.stack(
            [
                lax.ppermute(features[:, -1], "col", right),
                lax.ppermute(features[:, 0], "col", left),
            ]
        )
    rounds = [("row", 1 << k) for k in range(2, (rows - 1).bit_length())]
    rounds[1:1] = [("col", 1 << k) for k in range((cols - 1).bit_length())]
    rounds.append(("row", 2))
    mixed = {0: (4, 2), len(rounds) - 1: (2, 4)}
    middle = min(3, tile_rows - 1)
    work = [tuple(range(1, middle)), tuple(range(middle, tile_rows - 1)), ()]
    firsts, parts = [], []

    def next_work(given):
        targets = work.pop(0)
        halos = () if targets else (near_halo, far_halo, near_corner, far_corner)
        earlier = () if targets else tuple(parts)
        made = list(
            conv(targets, given, features, beside, halos, earlier, tuple(firsts), conv_weight, bias)
        )
        if not targets:
            return made
        firsts.append(targets[0])
        parts.extend(made)
        return made

    for turn, (axis, bit) in enumerate(rounds):
        pairs = swap(axis, bit)
        if turn in mixed:
            pairs = [(i, i ^ mixed[turn][i % 2]) for i in range(rows)]
        received = lax.ppermute(total, axis, pairs)
        if turn == 0:
            far_halo = lax.ppermute(together(far, total)[0], "row", next_chip)
            near = near_row(together(place, total)[0], features)
            received, near, beside = together(received, near, beside)
            near_halo = lax.ppermute(near, "row", swap("row", 1))
            near_corner = jnp.where(core == 0, beside[:, -1], beside[:, 0])
            far_corner = jnp.where(core == 0, beside[:, 0], beside[:, -1])
            near_corner = lax.ppermute(near_corner, "row", swap("row", 1))
            far_corner = lax.ppermute(far_corner, "row", next_chip)
        if turn == 1:
            received, near_halo, near_corner = together(received, near_halo, near_corner)
        if turn > 0 and work:
            made = next_work(together(where, total)[0])
            received, made[0] = together(received, made[0])
            if work:
                parts[-1] = made[0]
        if turn == 2:
            received, far_halo, far_corner = together(received, far_halo, far_corner)
        total = total + received
    rest = lax.ppermute(total, "row", swap("row", 1))
    while work:
        made = next_work(where)
    return tuple(attend(place, queries, total, rest, *made))


def solution(mesh):
    tiled = P("row", "col", None)
    return jax.shard_map(
        on_device,
        mesh=mesh,
        in_specs=(tiled, tiled, tiled, tiled, P(), P()),
        out_specs=(tiled, tiled),
        check_vma=False,
    )
```

time: 249 us -> 47.1 us (0.19)
  other arithmetic: 60.9 us -> 0.38 us
  waiting for transfers between devices: 55.4 us -> 3.13 us
  local copies, waits for them, and re-layouts: 53.1 us -> 2.68 us
  blocking collectives: 43.5 us -> 0 us
  Pallas kernels: 0 us -> 24.7 us
  between operations: 14.3 us -> 0.82 us
  matrix products: 10.4 us -> 0 us
  starting transfers between devices: 10.7 us -> 15.2 us
    psum x1 -> x0, waiting for transfers between devices: 55.4 us -> none  [on_device(): state_sum, key_sum = lax.psum((local_state, local_keys), ('row', 'col'))]
    psum x1 -> x0, blocking collectives: 43.5 us -> none  [on_device(): state_sum, key_sum = lax.psum((local_state, local_keys), ('row', 'col'))]
    add x2 -> x5, other arithmetic: 29.8 us -> 0.11 us  [the longest x4 0.09 us: on_device(): total = total + received]
    pallas_call x0 -> x6, Pallas kernels: none -> 24.7 us  [the longest x3 14.9 us: conv(): pl.pallas_call(functools.partial(conv_kernel, targets, firsts, unroll), o...]
    concatenate x1 -> x0, other arithmetic: 22.1 us -> none  [padded_2(): block = jnp.concatenate([low, block, high], axis=dim)]
    max x3 -> x0, local copies, waits for them, and re-layouts: 16.1 us -> none  [the longest x2 11 us: on_device(): jnp.maximum(queries.reshape(-1, HEADS, HEAD_DIM), 0).astype(jnp.float32)]
    unnamed x39 -> x10, local copies, waits for them, and re-layouts: 18.2 us -> 2.65 us
    reshape x3 -> x1, local copies, waits for them, and re-layouts: 11 us -> 0.03 us  [on_device(): bias = conv_bias.reshape(1, -1)]
  transfers between devices with their start and end apart: 5 -> 11, of which waited for: 1 -> 2; matrix products, arithmetic and copies ran while one was open for 25% -> 1% of each run, Pallas kernels for 0% -> 35%
where the time goes in v1:
time: 47.1 us; the launch traced here: 46.9 us
  Pallas kernels  24.7 us (52%)
  starting transfers between devices  15.2 us (32%)
  waiting for transfers between devices  3.13 us (7%)
  local copies, waits for them, and re-layouts  2.68 us (6%)
  between operations  0.82 us (2%)
    pallas_call x3, Pallas kernels, conv(): pl.pallas_call(functools.partial(conv_kernel, targets, firsts, unroll), o...  14.9 us
    ppermute x4, starting transfers between devices, on_device(): received = lax.ppermute(total, axis, pairs)  7.96 us
    pallas_call x1, Pallas kernels, local_state(): pl.pallas_call(functools.partial(state_kernel, channels), out_shape=shape...  4.87 us
    pallas_call x1, Pallas kernels, attend(): pl.pallas_call(functools.partial(attend_kernel, channels), out_shape=[jax...  3.46 us
    unnamed x10, local copies, waits for them, and re-layouts  2.65 us
    ppermute x1, starting transfers between devices, on_device(): beside = lax.ppermute(edges[0], 'col', swap('col', 1))[None]  2.56 us
    ppermute x1, starting transfers between devices, on_device(): near_halo = lax.ppermute(near, 'row', swap('row', 1))  2.56 us
    ppermute x4, waiting for transfers between devices, on_device(): received = lax.ppermute(total, axis, pairs)  1.75 us
  transfers between devices with their start and end apart: 11, of which 2 were waited for; matrix products, arithmetic and copies ran while one was open for 1% of the time, Pallas kernels for 35%

profile of v1, /device:TPU:0, one launch (start us, length us, event | category | flops | bytes accessed | tf_op | source)
XLA Modules:
  0.0 46.9 jit_solution(3701975004328658077)
XLA Ops:
  0.6 0.1 pad_add_fusion.place
  0.7 4.9 %local_state.1 = (f32[304,128]{1,0:T(8,128)S(1)}, f32[304,128]{1,0:T(8,128)S(1)}, bf16[1,32,11200]{2,1,0:T(8,128)(2,1)}, bf16[8,11200]{1,0:T(8,128)(2,1)S(1)}) custom-call(s32[2]{0:T(128)S(1)} %pad_add_fusion.place, bf16[8,32,2240]{2,1,0:T(8,128)(2,1)} %k_ref.1, bf16[8,32,2240]{2,1,0:T(8,128)(2,1)} %v_ref.1, bf16[8,32,11200]{2,1,0:T(8,128)(2,1)} %refs_1_.5), custom_call_target="tpu_custom_call" | custom-call | flops 536870912 | bytes 67108864 | tf_op jit(solution)/shard_map/local_state/pallas_call | solution.py:116
  5.6 0.5 %collective-permute-start = (f32[304,128]{1,0:T(8,128)S(1)}, f32[304,128]{1,0:T(8,128)S(1)}, u32[]{:S(2)}, u32[]{:S(2)}) collective-permute-start(f32[304,128]{1,0:T(8,128)S(1)} %get-tuple-element.29), channel_id=1, source_target_pairs={{0,2},{2,0},{4,6},{6,4},{8,10},{10,8},{12,14},{14,12},{16,18},{18,... | collective-permute-start | bytes 466952 | tf_op jit(solution)/shard_map/ppermute | solution.py:451
  6.1 2.6 %collective-permute-start.2 = (bf16[8,11200]{1,0:T(8,128)(2,1)S(1)}, bf16[8,11200]{1,0:T(8,128)(2,1)S(1)}, u32[]{:S(2)}, u32[]{:S(2)}) collective-permute-start(bf16[8,11200]{1,0:T(8,128)(2,1)S(1)} %get-tuple-element.31), channel_id=1, source_target_pairs={{0,1},{1,0},{2,3},{3,2},{4,5},{5,4},{6,7},{7,6},{8,9},{9,8},{10,11... | collective-permute-start | bytes 537608 | tf_op jit(solution)/shard_map/ppermute | solution.py:453
  8.7 0.0 collective-permute-done
  8.7 1.6 %collective-permute-start.1 = (f32[304,128]{1,0:T(8,128)S(1)}, f32[304,128]{1,0:T(8,128)S(1)}, u32[]{:S(2)}, u32[]{:S(2)}) collective-permute-start(f32[304,128]{1,0:T(8,128)S(1)} %add.20), channel_id=1, source_target_pairs={{0,8},{2,6},{4,12},{6,2},{8,0},{10,14},{12,4},{14,10},{16,24},{18,... | collective-permute-start | bytes 466952 | tf_op jit(solution)/shard_map/ppermute | solution.py:488
  10.3 0.0 copy-start
  10.3 2.6 %copy-done = bf16[8,32,11200]{2,1,0:T(8,128)(2,1)S(1)} copy-done((bf16[8,32,11200]{2,1,0:T(8,128)(2,1)S(1)}, bf16[8,32,11200]{2,1,0:T(8,128)(2,1)}, u32[]{:S(2)}) %copy-start) | copy-done | bytes 5734424
  13.0 0.0 copy-start.4
  13.0 0.0 copy-start.1
  13.0 0.0 copy-start.2
  13.0 1.4 %near_row.1 = bf16[1,32,11200]{2,1,0:T(8,128)(2,1)} custom-call(s32[2]{0:T(128)S(1)} %pad_add_fusion.place, bf16[8,32,11200]{2,1,0:T(8,128)(2,1)S(1)} %copy-done), custom_call_target="tpu_custom_call" | custom-call | flops 1024 | bytes 1024 | tf_op jit(solution)/shard_map/near_row/pallas_call | solution.py:419
  14.4 0.8 %collective-permute-start.7 = (bf16[1,32,11200]{2,1,0:T(8,128)(2,1)}, bf16[1,32,11200]{2,1,0:T(8,128)(2,1)S(1)}, u32[]{:S(2)}, u32[]{:S(2)}) collective-permute-start(bf16[1,32,11200]{2,1,0:T(8,128)(2,1)} %get-tuple-element.41), channel_id=1, source_target_pairs={{2,4},{6,8},{10,12},{14,16},{18,20},{22,24},{26,28},{4,2},{8,6},{1... | collective-permute-start | bytes 2150408 | tf_op jit(solution)/shard_map/ppermute | solution.py:490
  15.2 0.0 collective-permute-done.2
  15.3 0.0 collective-permute-done.1
  15.3 1.4 %collective-permute-start.3 = (f32[304,128]{1,0:T(8,128)S(1)}, f32[304,128]{1,0:T(8,128)S(1)}, u32[]{:S(2)}, u32[]{:S(2)}) collective-permute-start(f32[304,128]{1,0:T(8,128)S(1)} %add.21), channel_id=1, source_target_pairs={{0,1},{1,0},{2,3},{3,2},{4,5},{5,4},{6,7},{7,6},{8,9},{9,8},{10,11... | collective-permute-start | bytes 466952 | tf_op jit(solution)/shard_map/ppermute | solution.py:488
  16.7 2.6 %collective-permute-start.4 = (bf16[1,32,11200]{2,1,0:T(8,128)(2,1)}, bf16[1,32,11200]{2,1,0:T(8,128)(2,1)S(1)}, u32[]{:S(2)}, u32[]{:S(2)}) collective-permute-start(bf16[1,32,11200]{2,1,0:T(8,128)(2,1)} %near_row.1), channel_id=1, source_target_pairs={{0,2},{2,0},{4,6},{6,4},{8,10},{10,8},{12,14},{14,12},{16,18},{18,... | collective-permute-start | bytes 2150408 | tf_op jit(solution)/shard_map/ppermute | solution.py:493
  19.2 0.1 fusion.1
  19.3 0.1 collective-permute-start.5
  19.4 0.1 pad_add_fusion.1.refs_0_
  19.5 0.0 copy-done.4
  19.5 0.0 copy-done.1
  19.5 0.0 copy-done.2
  19.5 4.3 %conv_rows.2.refs_7_ = bf16[2,32,5600]{2,1,0:T(8,128)(2,1)S(1)} custom-call(s32[3]{0:T(128)S(1)} %pad_add_fusion.1.refs_0_, bf16[8,32,11200]{2,1,0:T(8,128)(2,1)S(1)} %copy-done.1, bf16[1,8,11200]{2,1,0:T(8,128)(2,1)S(1)} %bitcast.10, bf16[3,3,11200]{2,1,0:T(4,128)(2,1)S(1)} %copy-done.2, bf16[1,11200]{1,0:T(2,128)(2,1)S(1)} %reshape.51.refs_4_.refs_10_), custom_call_target="tpu_custom_call" | custom-call | flops 1024 | bytes 1024 | tf_op jit(solution)/shard_map/conv_rows/pallas_call | solution.py:399
  23.8 0.0 collective-permute-done.5.refs_5_
  23.8 0.0 collective-permute-done.3
  23.8 0.0 collective-permute-done.4.refs_3_
  23.9 2.7 %collective-permute-start.6 = (f32[304,128]{1,0:T(8,128)S(1)}, f32[304,128]{1,0:T(8,128)S(1)}, u32[]{:S(2)}, u32[]{:S(2)}) collective-permute-start(f32[304,128]{1,0:T(8,128)S(1)} %add.22), channel_id=1, source_target_pairs={{0,16},{2,18},{4,20},{6,22},{8,24},{10,26},{12,28},{14,30},{16,0},... | collective-permute-start | bytes 466952 | tf_op jit(solution)/shard_map/ppermute | solution.py:488
  26.5 0.7 %collective-permute-start.8 = (bf16[1,11200]{1,0:T(2,128)(2,1)S(1)}, bf16[1,11200]{1,0:T(2,128)(2,1)S(1)}, u32[]{:S(2)}, u32[]{:S(2)}) collective-permute-start(bf16[1,11200]{1,0:T(2,128)(2,1)S(1)} %get-tuple-element.54), channel_id=1, source_target_pairs={{2,4},{6,8},{10,12},{14,16},{18,20},{22,24},{26,28},{4,2},{8,6},{1... | collective-permute-start | bytes 67208 | tf_op jit(solution)/shard_map/ppermute | solution.py:497
  27.2 6.3 %conv_rows.3.refs_8_ = bf16[4,32,5600]{2,1,0:T(8,128)(2,1)S(1)} custom-call(s32[3]{0:T(128)S(1)} %pad_add_fusion.1.refs_0_, bf16[8,32,11200]{2,1,0:T(8,128)(2,1)S(1)} %copy-done.1, bf16[1,8,11200]{2,1,0:T(8,128)(2,1)S(1)} %bitcast.11, bf16[3,3,11200]{2,1,0:T(4,128)(2,1)S(1)} %copy-done.2, bf16[1,11200]{1,0:T(2,128)(2,1)S(1)} %reshape.51.refs_4_.refs_10_), custom_call_target="tpu_custom_call" | custom-call | flops 1024 | bytes 1024 | tf_op jit(solution)/shard_map/conv_rows/pallas_call | solution.py:399
  33.5 1.7 %collective-permute-done.6 = f32[304,128]{1,0:T(8,128)S(1)} collective-permute-done((f32[304,128]{1,0:T(8,128)S(1)}, f32[304,128]{1,0:T(8,128)S(1)}, u32[]{:S(2)}, u32[]{:S(2)}) %collective-permute-start.6) | collective-permute-done | bytes 155680 | tf_op jit(solution)/shard_map/ppermute | solution.py:488
  35.2 0.0 collective-permute-done.8.refs_6_
  35.2 0.0 collective-permute-done.7.refs_4_
  35.2 0.0 copy-start.3
  35.3 2.3 %collective-permute-start.9 = (f32[304,128]{1,0:T(8,128)S(1)}, f32[304,128]{1,0:T(8,128)S(1)}, u32[]{:S(2)}, u32[]{:S(2)}) collective-permute-start(f32[304,128]{1,0:T(8,128)S(1)} %add.23), channel_id=1, source_target_pairs={{0,4},{2,10},{4,0},{6,14},{8,12},{10,2},{12,8},{14,6},{16,20},{18,... | collective-permute-start | bytes 466952 | tf_op jit(solution)/shard_map/ppermute | solution.py:488
  37.6 4.4 %conv_ends.1 = (bf16[2,32,5600]{2,1,0:T(8,128)(2,1)S(1)}, bf16[8,32,5600]{2,1,0:T(8,128)(2,1)}) custom-call(s32[3]{0:T(128)S(1)} %pad_add_fusion.1.refs_0_, bf16[8,32,11200]{2,1,0:T(8,128)(2,1)S(1)} %copy-done.1, bf16[1,8,11200]{2,1,0:T(8,128)(2,1)S(1)} %bitcast.12, bf16[1,32,11200]{2,1,0:T(8,128)(2,1)S(1)} %collective-permute-done.4.refs_3_, ...), custom_call_target="tpu_custom_call" | custom-call | flops 1024 | bytes 1024 | tf_op jit(solution)/shard_map/conv_ends/pallas_call | solution.py:399
  42.0 0.0 collective-permute-done.9
  42.0 0.1 collective-permute-start.10
  42.1 1.4 %collective-permute-done.10.other = f32[304,128]{1,0:T(8,128)S(1)} collective-permute-done((f32[304,128]{1,0:T(8,128)S(1)}, f32[304,128]{1,0:T(8,128)S(1)}, u32[]{:S(2)}, u32[]{:S(2)}) %collective-permute-start.10) | collective-permute-done | bytes 155680 | tf_op jit(solution)/shard_map/ppermute | solution.py:508
  43.4 0.0 copy-done.3
  43.4 3.5 %attend.1 = (bf16[8,32,2240]{2,1,0:T(8,128)(2,1)}, bf16[8,32,5600]{2,1,0:T(8,128)(2,1)}) custom-call(s32[2]{0:T(128)S(1)} %pad_add_fusion.place, bf16[8,32,2240]{2,1,0:T(8,128)(2,1)S(1)} %copy-done.3, f32[304,128]{1,0:T(8,128)S(1)} %add.24.mine, f32[304,128]{1,0:T(8,128)S(1)} %collective-permute-done.10.other, ...), custom_call_target="tpu_custom_call", output_to_operand_aliasing={{1}: (5, {})} | custom-call | flops 1024 | bytes 1024 | tf_op jit(solution)/shard_map/attend/pallas_call | solution.py:203
  (6 shorter events, 0.1 us)
Async XLA Ops:
  5.6 3.1 %collective-permute-start = (f32[304,128]{1,0:T(8,128)S(1)}, f32[304,128]{1,0:T(8,128)S(1)}, u32[]{:S(2)}, u32[]{:S(2)}) collective-permute-start(f32[304,128]{1,0:T(8,128)S(1)} %get-tuple-element.29), channel_id=1, source_target_pairs={{0,2},{2,0},{4,6},{6,4},{8,10},{10,8},{12,14},{14,12},{16,18},{18,... | collective-permute-start | bytes 466952 | tf_op jit(solution)/shard_map/ppermute | solution.py:451
  6.1 9.1 %collective-permute-start.2 = (bf16[8,11200]{1,0:T(8,128)(2,1)S(1)}, bf16[8,11200]{1,0:T(8,128)(2,1)S(1)}, u32[]{:S(2)}, u32[]{:S(2)}) collective-permute-start(bf16[8,11200]{1,0:T(8,128)(2,1)S(1)} %get-tuple-element.31), channel_id=1, source_target_pairs={{0,1},{1,0},{2,3},{3,2},{4,5},{5,4},{6,7},{7,6},{8,9},{9,8},{10,11... | collective-permute-start | bytes 537608 | tf_op jit(solution)/shard_map/ppermute | solution.py:453
  8.7 6.6 %collective-permute-start.1 = (f32[304,128]{1,0:T(8,128)S(1)}, f32[304,128]{1,0:T(8,128)S(1)}, u32[]{:S(2)}, u32[]{:S(2)}) collective-permute-start(f32[304,128]{1,0:T(8,128)S(1)} %add.20), channel_id=1, source_target_pairs={{0,8},{2,6},{4,12},{6,2},{8,0},{10,14},{12,4},{14,10},{16,24},{18,... | collective-permute-start | bytes 466952 | tf_op jit(solution)/shard_map/ppermute | solution.py:488
  10.3 2.6 %copy-start = (bf16[8,32,11200]{2,1,0:T(8,128)(2,1)S(1)}, bf16[8,32,11200]{2,1,0:T(8,128)(2,1)}, u32[]{:S(2)}) copy-start(bf16[8,32,11200]{2,1,0:T(8,128)(2,1)} %refs_1_.5) | copy-start | bytes 17203204
  13.0 6.5 %copy-start.4 = (bf16[11200]{0:T(1024)(128)(2,1)S(1)}, bf16[11200]{0:T(1024)(128)(2,1)}, u32[]{:S(2)}) copy-start(bf16[11200]{0:T(1024)(128)(2,1)} %param.11) | copy-start | bytes 67204
  13.0 6.5 %copy-start.1 = (bf16[8,32,11200]{2,1,0:T(8,128)(2,1)S(1)}, bf16[8,32,11200]{2,1,0:T(8,128)(2,1)}, u32[]{:S(2)}) copy-start(bf16[8,32,11200]{2,1,0:T(8,128)(2,1)} %refs_1_.5) | copy-start | bytes 17203204
  13.0 6.6 %copy-start.2 = (bf16[3,3,11200]{2,1,0:T(4,128)(2,1)S(1)}, bf16[3,3,11200]{2,1,0:T(4,128)(2,1)}, u32[]{:S(2)}) copy-start(bf16[3,3,11200]{2,1,0:T(4,128)(2,1)} %refs_9_.1) | copy-start | bytes 604804
  14.4 20.8 %collective-permute-start.7 = (bf16[1,32,11200]{2,1,0:T(8,128)(2,1)}, bf16[1,32,11200]{2,1,0:T(8,128)(2,1)S(1)}, u32[]{:S(2)}, u32[]{:S(2)}) collective-permute-start(bf16[1,32,11200]{2,1,0:T(8,128)(2,1)} %get-tuple-element.41), channel_id=1, source_target_pairs={{2,4},{6,8},{10,12},{14,16},{18,20},{22,24},{26,28},{4,2},{8,6},{1... | collective-permute-start | bytes 2150408 | tf_op jit(solution)/shard_map/ppermute | solution.py:490
  15.3 8.5 %collective-permute-start.3 = (f32[304,128]{1,0:T(8,128)S(1)}, f32[304,128]{1,0:T(8,128)S(1)}, u32[]{:S(2)}, u32[]{:S(2)}) collective-permute-start(f32[304,128]{1,0:T(8,128)S(1)} %add.21), channel_id=1, source_target_pairs={{0,1},{1,0},{2,3},{3,2},{4,5},{5,4},{6,7},{7,6},{8,9},{9,8},{10,11... | collective-permute-start | bytes 466952 | tf_op jit(solution)/shard_map/ppermute | solution.py:488
  16.7 7.2 %collective-permute-start.4 = (bf16[1,32,11200]{2,1,0:T(8,128)(2,1)}, bf16[1,32,11200]{2,1,0:T(8,128)(2,1)S(1)}, u32[]{:S(2)}, u32[]{:S(2)}) collective-permute-start(bf16[1,32,11200]{2,1,0:T(8,128)(2,1)} %near_row.1), channel_id=1, source_target_pairs={{0,2},{2,0},{4,6},{6,4},{8,10},{10,8},{12,14},{14,12},{16,18},{18,... | collective-permute-start | bytes 2150408 | tf_op jit(solution)/shard_map/ppermute | solution.py:493
  19.3 4.5 %collective-permute-start.5 = (bf16[1,11200]{1,0:T(2,128)(2,1)S(1)}, bf16[1,11200]{1,0:T(2,128)(2,1)S(1)}, u32[]{:S(2)}, u32[]{:S(2)}) collective-permute-start(bf16[1,11200]{1,0:T(2,128)(2,1)S(1)} %get-tuple-element.55), channel_id=1, source_target_pairs={{0,2},{2,0},{4,6},{6,4},{8,10},{10,8},{12,14},{14,12},{16,18},{18,... | collective-permute-start | bytes 67208 | tf_op jit(solution)/shard_map/ppermute | solution.py:496
  23.9 11.4 %collective-permute-start.6 = (f32[304,128]{1,0:T(8,128)S(1)}, f32[304,128]{1,0:T(8,128)S(1)}, u32[]{:S(2)}, u32[]{:S(2)}) collective-permute-start(f32[304,128]{1,0:T(8,128)S(1)} %add.22), channel_id=1, source_target_pairs={{0,16},{2,18},{4,20},{6,22},{8,24},{10,26},{12,28},{14,30},{16,0},... | collective-permute-start | bytes 466952 | tf_op jit(solution)/shard_map/ppermute | solution.py:488
  26.5 8.7 %collective-permute-start.8 = (bf16[1,11200]{1,0:T(2,128)(2,1)S(1)}, bf16[1,11200]{1,0:T(2,128)(2,1)S(1)}, u32[]{:S(2)}, u32[]{:S(2)}) collective-permute-start(bf16[1,11200]{1,0:T(2,128)(2,1)S(1)} %get-tuple-element.54), channel_id=1, source_target_pairs={{2,4},{6,8},{10,12},{14,16},{18,20},{22,24},{26,28},{4,2},{8,6},{1... | collective-permute-start | bytes 67208 | tf_op jit(solution)/shard_map/ppermute | solution.py:497
  35.2 8.2 %copy-start.3 = (bf16[8,32,2240]{2,1,0:T(8,128)(2,1)S(1)}, bf16[8,32,2240]{2,1,0:T(8,128)(2,1)}, u32[]{:S(2)}) copy-start(bf16[8,32,2240]{2,1,0:T(8,128)(2,1)} %q_ref.1) | copy-start | bytes 3440644
  35.3 6.7 %collective-permute-start.9 = (f32[304,128]{1,0:T(8,128)S(1)}, f32[304,128]{1,0:T(8,128)S(1)}, u32[]{:S(2)}, u32[]{:S(2)}) collective-permute-start(f32[304,128]{1,0:T(8,128)S(1)} %add.23), channel_id=1, source_target_pairs={{0,4},{2,10},{4,0},{6,14},{8,12},{10,2},{12,8},{14,6},{16,20},{18,... | collective-permute-start | bytes 466952 | tf_op jit(solution)/shard_map/ppermute | solution.py:488
  42.0 1.4 %collective-permute-start.10 = (f32[304,128]{1,0:T(8,128)S(1)}, f32[304,128]{1,0:T(8,128)S(1)}, u32[]{:S(2)}, u32[]{:S(2)}) collective-permute-start(f32[304,128]{1,0:T(8,128)S(1)} %add.24.mine), channel_id=1, source_target_pairs={{0,2},{2,0},{4,6},{6,4},{8,10},{10,8},{12,14},{14,12},{16,18},{18,... | collective-permute-start | bytes 466952 | tf_op jit(solution)/shard_map/ppermute | solution.py:508

commit v2 on v1

--- a/solution.py
+++ b/solution.py
@@ -464,7 +464,7 @@
     rounds[1:1] = [("col", 1 << k) for k in range((cols - 1).bit_length())]
     rounds.append(("row", 2))
     mixed = {0: (4, 2), len(rounds) - 1: (2, 4)}
-    middle = min(3, tile_rows - 1)
+    middle = min(4, tile_rows - 1)
     work = [tuple(range(1, middle)), tuple(range(middle, tile_rows - 1)), ()]
     firsts, parts = [], []
 

time: 47.1 us -> 47.1 us (level)
  waiting for transfers between devices: 3.13 us -> 3.73 us
    ppermute x4, waiting for transfers between devices: 1.75 us -> 2.35 us  [on_device(): received = lax.ppermute(total, axis, pairs)]
  transfers between devices with their start and end apart: 11 -> 11, of which waited for: 2 -> 2; matrix products, arithmetic and copies ran while one was open for 1% -> 1% of each run, Pallas kernels for 35% -> 34%
where the time goes in v2:
time: 47.1 us; the launch traced here: 46.9 us
  Pallas kernels  24.3 us (52%)
  starting transfers between devices  15 us (32%)
  waiting for transfers between devices  3.73 us (8%)
  local copies, waits for them, and re-layouts  2.68 us (6%)
  between operations  0.81 us (2%)
    pallas_call x3, Pallas kernels, conv(): pl.pallas_call(functools.partial(conv_kernel, targets, firsts, unroll), o...  14.6 us
    ppermute x4, starting transfers between devices, on_device(): received = lax.ppermute(total, axis, pairs)  7.72 us
    pallas_call x1, Pallas kernels, local_state(): pl.pallas_call(functools.partial(state_kernel, channels), out_shape=shape...  4.87 us
    pallas_call x1, Pallas kernels, attend(): pl.pallas_call(functools.partial(attend_kernel, channels), out_shape=[jax...  3.46 us
    unnamed x10, local copies, waits for them, and re-layouts  2.65 us
    ppermute x1, starting transfers between devices, on_device(): beside = lax.ppermute(edges[0], 'col', swap('col', 1))[None]  2.56 us
    ppermute x1, starting transfers between devices, on_device(): near_halo = lax.ppermute(near, 'row', swap('row', 1))  2.56 us
    ppermute x4, waiting for transfers between devices, on_device(): received = lax.ppermute(total, axis, pairs)  2.35 us
  transfers between devices with their start and end apart: 11, of which 2 were waited for; matrix products, arithmetic and copies ran while one was open for 1% of the time, Pallas kernels for 34%

profile of v2, /device:TPU:0, one launch (start us, length us, event | category | flops | bytes accessed | tf_op | source)
XLA Modules:
  0.0 46.9 jit_solution(7002085495709612159)
XLA Ops:
  0.6 0.1 pad_add_fusion.place
  0.7 4.9 %local_state.1 = (f32[304,128]{1,0:T(8,128)S(1)}, f32[304,128]{1,0:T(8,128)S(1)}, bf16[1,32,11200]{2,1,0:T(8,128)(2,1)}, bf16[8,11200]{1,0:T(8,128)(2,1)S(1)}) custom-call(s32[2]{0:T(128)S(1)} %pad_add_fusion.place, bf16[8,32,2240]{2,1,0:T(8,128)(2,1)} %k_ref.1, bf16[8,32,2240]{2,1,0:T(8,128)(2,1)} %v_ref.1, bf16[8,32,11200]{2,1,0:T(8,128)(2,1)} %refs_1_.5), custom_call_target="tpu_custom_call" | custom-call | flops 536870912 | bytes 67108864 | tf_op jit(solution)/shard_map/local_state/pallas_call | solution.py:116
  5.6 0.5 %collective-permute-start = (f32[304,128]{1,0:T(8,128)S(1)}, f32[304,128]{1,0:T(8,128)S(1)}, u32[]{:S(2)}, u32[]{:S(2)}) collective-permute-start(f32[304,128]{1,0:T(8,128)S(1)} %get-tuple-element.29), channel_id=1, source_target_pairs={{0,2},{2,0},{4,6},{6,4},{8,10},{10,8},{12,14},{14,12},{16,18},{18,... | collective-permute-start | bytes 466952 | tf_op jit(solution)/shard_map/ppermute | solution.py:451
  6.1 2.6 %collective-permute-start.2 = (bf16[8,11200]{1,0:T(8,128)(2,1)S(1)}, bf16[8,11200]{1,0:T(8,128)(2,1)S(1)}, u32[]{:S(2)}, u32[]{:S(2)}) collective-permute-start(bf16[8,11200]{1,0:T(8,128)(2,1)S(1)} %get-tuple-element.31), channel_id=1, source_target_pairs={{0,1},{1,0},{2,3},{3,2},{4,5},{5,4},{6,7},{7,6},{8,9},{9,8},{10,11... | collective-permute-start | bytes 537608 | tf_op jit(solution)/shard_map/ppermute | solution.py:453
  8.7 0.0 collective-permute-done
  8.7 1.6 %collective-permute-start.1 = (f32[304,128]{1,0:T(8,128)S(1)}, f32[304,128]{1,0:T(8,128)S(1)}, u32[]{:S(2)}, u32[]{:S(2)}) collective-permute-start(f32[304,128]{1,0:T(8,128)S(1)} %add.20), channel_id=1, source_target_pairs={{0,8},{2,6},{4,12},{6,2},{8,0},{10,14},{12,4},{14,10},{16,24},{18,... | collective-permute-start | bytes 466952 | tf_op jit(solution)/shard_map/ppermute | solution.py:488
  10.3 0.0 copy-start
  10.3 2.6 %copy-done = bf16[8,32,11200]{2,1,0:T(8,128)(2,1)S(1)} copy-done((bf16[8,32,11200]{2,1,0:T(8,128)(2,1)S(1)}, bf16[8,32,11200]{2,1,0:T(8,128)(2,1)}, u32[]{:S(2)}) %copy-start) | copy-done | bytes 5734424
  13.0 0.0 copy-start.4
  13.0 0.0 copy-start.1
  13.0 0.0 copy-start.2
  13.0 1.4 %near_row.1 = bf16[1,32,11200]{2,1,0:T(8,128)(2,1)} custom-call(s32[2]{0:T(128)S(1)} %pad_add_fusion.place, bf16[8,32,11200]{2,1,0:T(8,128)(2,1)S(1)} %copy-done), custom_call_target="tpu_custom_call" | custom-call | flops 1024 | bytes 1024 | tf_op jit(solution)/shard_map/near_row/pallas_call | solution.py:419
  14.4 0.8 %collective-permute-start.7 = (bf16[1,32,11200]{2,1,0:T(8,128)(2,1)}, bf16[1,32,11200]{2,1,0:T(8,128)(2,1)S(1)}, u32[]{:S(2)}, u32[]{:S(2)}) collective-permute-start(bf16[1,32,11200]{2,1,0:T(8,128)(2,1)} %get-tuple-element.41), channel_id=1, source_target_pairs={{2,4},{6,8},{10,12},{14,16},{18,20},{22,24},{26,28},{4,2},{8,6},{1... | collective-permute-start | bytes 2150408 | tf_op jit(solution)/shard_map/ppermute | solution.py:490
  15.2 0.0 collective-permute-done.2
  15.3 0.0 collective-permute-done.1
  15.3 1.4 %collective-permute-start.3 = (f32[304,128]{1,0:T(8,128)S(1)}, f32[304,128]{1,0:T(8,128)S(1)}, u32[]{:S(2)}, u32[]{:S(2)}) collective-permute-start(f32[304,128]{1,0:T(8,128)S(1)} %add.21), channel_id=1, source_target_pairs={{0,1},{1,0},{2,3},{3,2},{4,5},{5,4},{6,7},{7,6},{8,9},{9,8},{10,11... | collective-permute-start | bytes 466952 | tf_op jit(solution)/shard_map/ppermute | solution.py:488
  16.7 2.6 %collective-permute-start.4 = (bf16[1,32,11200]{2,1,0:T(8,128)(2,1)}, bf16[1,32,11200]{2,1,0:T(8,128)(2,1)S(1)}, u32[]{:S(2)}, u32[]{:S(2)}) collective-permute-start(bf16[1,32,11200]{2,1,0:T(8,128)(2,1)} %near_row.1), channel_id=1, source_target_pairs={{0,2},{2,0},{4,6},{6,4},{8,10},{10,8},{12,14},{14,12},{16,18},{18,... | collective-permute-start | bytes 2150408 | tf_op jit(solution)/shard_map/ppermute | solution.py:493
  19.2 0.1 fusion.1
  19.3 0.1 collective-permute-start.5
  19.4 0.1 pad_add_fusion.1.refs_0_
  19.5 0.0 copy-done.4
  19.5 0.0 copy-done.1
  19.5 0.0 copy-done.2
  19.5 5.1 %conv_rows.2.refs_7_ = bf16[3,32,5600]{2,1,0:T(8,128)(2,1)S(1)} custom-call(s32[3]{0:T(128)S(1)} %pad_add_fusion.1.refs_0_, bf16[8,32,11200]{2,1,0:T(8,128)(2,1)S(1)} %copy-done.1, bf16[1,8,11200]{2,1,0:T(8,128)(2,1)S(1)} %bitcast.10, bf16[3,3,11200]{2,1,0:T(4,128)(2,1)S(1)} %copy-done.2, bf16[1,11200]{1,0:T(2,128)(2,1)S(1)} %reshape.51.refs_4_.refs_10_), custom_call_target="tpu_custom_call" | custom-call | flops 1024 | bytes 1024 | tf_op jit(solution)/shard_map/conv_rows/pallas_call | solution.py:399
  24.6 0.0 collective-permute-done.5.refs_5_
  24.6 0.0 collective-permute-done.3
  24.6 0.0 collective-permute-done.4.refs_3_
  24.7 2.7 %collective-permute-start.6 = (f32[304,128]{1,0:T(8,128)S(1)}, f32[304,128]{1,0:T(8,128)S(1)}, u32[]{:S(2)}, u32[]{:S(2)}) collective-permute-start(f32[304,128]{1,0:T(8,128)S(1)} %add.22), channel_id=1, source_target_pairs={{0,16},{2,18},{4,20},{6,22},{8,24},{10,26},{12,28},{14,30},{16,0},... | collective-permute-start | bytes 466952 | tf_op jit(solution)/shard_map/ppermute | solution.py:488
  27.3 0.7 %collective-permute-start.8 = (bf16[1,11200]{1,0:T(2,128)(2,1)S(1)}, bf16[1,11200]{1,0:T(2,128)(2,1)S(1)}, u32[]{:S(2)}, u32[]{:S(2)}) collective-permute-start(bf16[1,11200]{1,0:T(2,128)(2,1)S(1)} %get-tuple-element.54), channel_id=1, source_target_pairs={{2,4},{6,8},{10,12},{14,16},{18,20},{22,24},{26,28},{4,2},{8,6},{1... | collective-permute-start | bytes 67208 | tf_op jit(solution)/shard_map/ppermute | solution.py:497
  28.0 5.1 %conv_rows.3.refs_8_ = bf16[3,32,5600]{2,1,0:T(8,128)(2,1)S(1)} custom-call(s32[3]{0:T(128)S(1)} %pad_add_fusion.1.refs_0_, bf16[8,32,11200]{2,1,0:T(8,128)(2,1)S(1)} %copy-done.1, bf16[1,8,11200]{2,1,0:T(8,128)(2,1)S(1)} %bitcast.11, bf16[3,3,11200]{2,1,0:T(4,128)(2,1)S(1)} %copy-done.2, bf16[1,11200]{1,0:T(2,128)(2,1)S(1)} %reshape.51.refs_4_.refs_10_), custom_call_target="tpu_custom_call" | custom-call | flops 1024 | bytes 1024 | tf_op jit(solution)/shard_map/conv_rows/pallas_call | solution.py:399
  33.1 2.3 %collective-permute-done.6 = f32[304,128]{1,0:T(8,128)S(1)} collective-permute-done((f32[304,128]{1,0:T(8,128)S(1)}, f32[304,128]{1,0:T(8,128)S(1)}, u32[]{:S(2)}, u32[]{:S(2)}) %collective-permute-start.6) | collective-permute-done | bytes 155680 | tf_op jit(solution)/shard_map/ppermute | solution.py:488
  35.5 0.0 collective-permute-done.8.refs_6_
  35.5 0.0 collective-permute-done.7.refs_4_
  35.5 2.1 %collective-permute-start.9 = (f32[304,128]{1,0:T(8,128)S(1)}, f32[304,128]{1,0:T(8,128)S(1)}, u32[]{:S(2)}, u32[]{:S(2)}) collective-permute-start(f32[304,128]{1,0:T(8,128)S(1)} %add.23), channel_id=1, source_target_pairs={{0,4},{2,10},{4,0},{6,14},{8,12},{10,2},{12,8},{14,6},{16,20},{18,... | collective-permute-start | bytes 466952 | tf_op jit(solution)/shard_map/ppermute | solution.py:488
  37.5 0.0 copy-start.3
  37.6 4.4 %conv_ends.1 = (bf16[2,32,5600]{2,1,0:T(8,128)(2,1)S(1)}, bf16[8,32,5600]{2,1,0:T(8,128)(2,1)}) custom-call(s32[3]{0:T(128)S(1)} %pad_add_fusion.1.refs_0_, bf16[8,32,11200]{2,1,0:T(8,128)(2,1)S(1)} %copy-done.1, bf16[1,8,11200]{2,1,0:T(8,128)(2,1)S(1)} %bitcast.12, bf16[1,32,11200]{2,1,0:T(8,128)(2,1)S(1)} %collective-permute-done.4.refs_3_, ...), custom_call_target="tpu_custom_call" | custom-call | flops 1024 | bytes 1024 | tf_op jit(solution)/shard_map/conv_ends/pallas_call | solution.py:399
  41.9 0.0 collective-permute-done.9
  42.0 0.1 collective-permute-start.10
  42.1 1.4 %collective-permute-done.10.other = f32[304,128]{1,0:T(8,128)S(1)} collective-permute-done((f32[304,128]{1,0:T(8,128)S(1)}, f32[304,128]{1,0:T(8,128)S(1)}, u32[]{:S(2)}, u32[]{:S(2)}) %collective-permute-start.10) | collective-permute-done | bytes 155680 | tf_op jit(solution)/shard_map/ppermute | solution.py:508
  43.4 0.0 copy-done.3
  43.4 3.5 %attend.1 = (bf16[8,32,2240]{2,1,0:T(8,128)(2,1)}, bf16[8,32,5600]{2,1,0:T(8,128)(2,1)}) custom-call(s32[2]{0:T(128)S(1)} %pad_add_fusion.place, bf16[8,32,2240]{2,1,0:T(8,128)(2,1)S(1)} %copy-done.3, f32[304,128]{1,0:T(8,128)S(1)} %add.24.mine, f32[304,128]{1,0:T(8,128)S(1)} %collective-permute-done.10.other, ...), custom_call_target="tpu_custom_call", output_to_operand_aliasing={{1}: (5, {})} | custom-call | flops 1024 | bytes 1024 | tf_op jit(solution)/shard_map/attend/pallas_call | solution.py:203
  (6 shorter events, 0.1 us)
Async XLA Ops:
  5.6 3.1 %collective-permute-start = (f32[304,128]{1,0:T(8,128)S(1)}, f32[304,128]{1,0:T(8,128)S(1)}, u32[]{:S(2)}, u32[]{:S(2)}) collective-permute-start(f32[304,128]{1,0:T(8,128)S(1)} %get-tuple-element.29), channel_id=1, source_target_pairs={{0,2},{2,0},{4,6},{6,4},{8,10},{10,8},{12,14},{14,12},{16,18},{18,... | collective-permute-start | bytes 466952 | tf_op jit(solution)/shard_map/ppermute | solution.py:451
  6.1 9.1 %collective-permute-start.2 = (bf16[8,11200]{1,0:T(8,128)(2,1)S(1)}, bf16[8,11200]{1,0:T(8,128)(2,1)S(1)}, u32[]{:S(2)}, u32[]{:S(2)}) collective-permute-start(bf16[8,11200]{1,0:T(8,128)(2,1)S(1)} %get-tuple-element.31), channel_id=1, source_target_pairs={{0,1},{1,0},{2,3},{3,2},{4,5},{5,4},{6,7},{7,6},{8,9},{9,8},{10,11... | collective-permute-start | bytes 537608 | tf_op jit(solution)/shard_map/ppermute | solution.py:453
  8.7 6.6 %collective-permute-start.1 = (f32[304,128]{1,0:T(8,128)S(1)}, f32[304,128]{1,0:T(8,128)S(1)}, u32[]{:S(2)}, u32[]{:S(2)}) collective-permute-start(f32[304,128]{1,0:T(8,128)S(1)} %add.20), channel_id=1, source_target_pairs={{0,8},{2,6},{4,12},{6,2},{8,0},{10,14},{12,4},{14,10},{16,24},{18,... | collective-permute-start | bytes 466952 | tf_op jit(solution)/shard_map/ppermute | solution.py:488
  10.3 2.6 %copy-start = (bf16[8,32,11200]{2,1,0:T(8,128)(2,1)S(1)}, bf16[8,32,11200]{2,1,0:T(8,128)(2,1)}, u32[]{:S(2)}) copy-start(bf16[8,32,11200]{2,1,0:T(8,128)(2,1)} %refs_1_.5) | copy-start | bytes 17203204
  13.0 6.5 %copy-start.4 = (bf16[11200]{0:T(1024)(128)(2,1)S(1)}, bf16[11200]{0:T(1024)(128)(2,1)}, u32[]{:S(2)}) copy-start(bf16[11200]{0:T(1024)(128)(2,1)} %param.11) | copy-start | bytes 67204
  13.0 6.5 %copy-start.1 = (bf16[8,32,11200]{2,1,0:T(8,128)(2,1)S(1)}, bf16[8,32,11200]{2,1,0:T(8,128)(2,1)}, u32[]{:S(2)}) copy-start(bf16[8,32,11200]{2,1,0:T(8,128)(2,1)} %refs_1_.5) | copy-start | bytes 17203204
  13.0 6.6 %copy-start.2 = (bf16[3,3,11200]{2,1,0:T(4,128)(2,1)S(1)}, bf16[3,3,11200]{2,1,0:T(4,128)(2,1)}, u32[]{:S(2)}) copy-start(bf16[3,3,11200]{2,1,0:T(4,128)(2,1)} %refs_9_.1) | copy-start | bytes 604804
  14.4 21.1 %collective-permute-start.7 = (bf16[1,32,11200]{2,1,0:T(8,128)(2,1)}, bf16[1,32,11200]{2,1,0:T(8,128)(2,1)S(1)}, u32[]{:S(2)}, u32[]{:S(2)}) collective-permute-start(bf16[1,32,11200]{2,1,0:T(8,128)(2,1)} %get-tuple-element.41), channel_id=1, source_target_pairs={{2,4},{6,8},{10,12},{14,16},{18,20},{22,24},{26,28},{4,2},{8,6},{1... | collective-permute-start | bytes 2150408 | tf_op jit(solution)/shard_map/ppermute | solution.py:490
  15.3 9.3 %collective-permute-start.3 = (f32[304,128]{1,0:T(8,128)S(1)}, f32[304,128]{1,0:T(8,128)S(1)}, u32[]{:S(2)}, u32[]{:S(2)}) collective-permute-start(f32[304,128]{1,0:T(8,128)S(1)} %add.21), channel_id=1, source_target_pairs={{0,1},{1,0},{2,3},{3,2},{4,5},{5,4},{6,7},{7,6},{8,9},{9,8},{10,11... | collective-permute-start | bytes 466952 | tf_op jit(solution)/shard_map/ppermute | solution.py:488
  16.7 8.0 %collective-permute-start.4 = (bf16[1,32,11200]{2,1,0:T(8,128)(2,1)}, bf16[1,32,11200]{2,1,0:T(8,128)(2,1)S(1)}, u32[]{:S(2)}, u32[]{:S(2)}) collective-permute-start(bf16[1,32,11200]{2,1,0:T(8,128)(2,1)} %near_row.1), channel_id=1, source_target_pairs={{0,2},{2,0},{4,6},{6,4},{8,10},{10,8},{12,14},{14,12},{16,18},{18,... | collective-permute-start | bytes 2150408 | tf_op jit(solution)/shard_map/ppermute | solution.py:493
  19.3 5.3 %collective-permute-start.5 = (bf16[1,11200]{1,0:T(2,128)(2,1)S(1)}, bf16[1,11200]{1,0:T(2,128)(2,1)S(1)}, u32[]{:S(2)}, u32[]{:S(2)}) collective-permute-start(bf16[1,11200]{1,0:T(2,128)(2,1)S(1)} %get-tuple-element.55), channel_id=1, source_target_pairs={{0,2},{2,0},{4,6},{6,4},{8,10},{10,8},{12,14},{14,12},{16,18},{18,... | collective-permute-start | bytes 67208 | tf_op jit(solution)/shard_map/ppermute | solution.py:496
  24.7 10.8 %collective-permute-start.6 = (f32[304,128]{1,0:T(8,128)S(1)}, f32[304,128]{1,0:T(8,128)S(1)}, u32[]{:S(2)}, u32[]{:S(2)}) collective-permute-start(f32[304,128]{1,0:T(8,128)S(1)} %add.22), channel_id=1, source_target_pairs={{0,16},{2,18},{4,20},{6,22},{8,24},{10,26},{12,28},{14,30},{16,0},... | collective-permute-start | bytes 466952 | tf_op jit(solution)/shard_map/ppermute | solution.py:488
  27.3 8.1 %collective-permute-start.8 = (bf16[1,11200]{1,0:T(2,128)(2,1)S(1)}, bf16[1,11200]{1,0:T(2,128)(2,1)S(1)}, u32[]{:S(2)}, u32[]{:S(2)}) collective-permute-start(bf16[1,11200]{1,0:T(2,128)(2,1)S(1)} %get-tuple-element.54), channel_id=1, source_target_pairs={{2,4},{6,8},{10,12},{14,16},{18,20},{22,24},{26,28},{4,2},{8,6},{1... | collective-permute-start | bytes 67208 | tf_op jit(solution)/shard_map/ppermute | solution.py:497
  35.5 6.5 %collective-permute-start.9 = (f32[304,128]{1,0:T(8,128)S(1)}, f32[304,128]{1,0:T(8,128)S(1)}, u32[]{:S(2)}, u32[]{:S(2)}) collective-permute-start(f32[304,128]{1,0:T(8,128)S(1)} %add.23), channel_id=1, source_target_pairs={{0,4},{2,10},{4,0},{6,14},{8,12},{10,2},{12,8},{14,6},{16,20},{18,... | collective-permute-start | bytes 466952 | tf_op jit(solution)/shard_map/ppermute | solution.py:488
  37.5 5.9 %copy-start.3 = (bf16[8,32,2240]{2,1,0:T(8,128)(2,1)S(1)}, bf16[8,32,2240]{2,1,0:T(8,128)(2,1)}, u32[]{:S(2)}) copy-start(bf16[8,32,2240]{2,1,0:T(8,128)(2,1)} %q_ref.1) | copy-start | bytes 3440644
  42.0 1.4 %collective-permute-start.10 = (f32[304,128]{1,0:T(8,128)S(1)}, f32[304,128]{1,0:T(8,128)S(1)}, u32[]{:S(2)}, u32[]{:S(2)}) collective-permute-start(f32[304,128]{1,0:T(8,128)S(1)} %add.24.mine), channel_id=1, source_target_pairs={{0,2},{2,0},{4,6},{6,4},{8,10},{10,8},{12,14},{14,12},{16,18},{18,... | collective-permute-start | bytes 466952 | tf_op jit(solution)/shard_map/ppermute | solution.py:508
